TPU v7x, 32 devices: a whole 2x2x4 slice. The times are simulated.
32 devices in a mesh: row: 8 (over z, x), col: 4 (over y, core).
Axes of the slice: x: 2, y: 2, z: 4, core: 2. Of those that a mesh axis runs over, the one named last changes fastest.
Arguments:
- hamiltonian: float32 [16384, 16384], P('row', 'col'), may hold values from -64 to 64, as said below
Outputs:
- updated: float32 [16384, 16384], P('row', 'col')
Inputs may be any that keep to these rules, and one draw needn't show every extreme that they name: hamiltonian is symmetric as a matrix in natural order.
All inputs are finite; a program needn't handle non-finite values.
Results may differ from a plain program's by a relative error of at most 0.0001.
Values sent between devices are 32-bit elements; how exact they have to be, the bound alone decides.
No kernel may reach another device: no remote copies, remote signals or barrier semaphores. Data moves between devices by JAX's collectives and lax.ppermute only.
A program may use at most 192 MiB of HBM per device.

v0:
```python
import jax
import jax.numpy as jnp
from jax import lax
from jax.experimental import pallas as pl
from jax.experimental.pallas import tpu as pltpu
from jax.sharding import PartitionSpec as P

NB = 128
PANELS = 2
CORES = 2
GROUP = 8
HIGH = lax.Precision.HIGHEST
BF16 = jnp.bfloat16
F32 = jnp.float32
AXES = ("row", "col")


def contract(left, right, left_dim, right_dim):
    return lax.dot_general(left, right, (((left_dim,), (right_dim,)), ((), ())), precision=HIGH)


def tile_rows(rows):
    return 512 if rows % 512 == 0 else rows


def halves(value):
    high = value.astype(BF16)
    return high, (value - high.astype(F32)).astype(BF16)


def product_kernel(a_ref, p_ref, *refs):
    out_ref, both = refs[-2:]

    @pl.when(pl.program_id(0) == 0)
    def _():
        high, low = halves(p_ref[...])
        both[:, :NB] = high
        both[:, NB:] = low

    high, low = halves(a_ref[...])
    p = both[...]
    total = jnp.dot(high, p, preferred_element_type=F32) + jnp.dot(low, p, preferred_element_type=F32)
    total = total[:, :NB] + total[:, NB:]
    out_ref[...] = total if len(refs) == 2 else refs[0][...] + total


def product(matrix, panel, index, before=()):
    rows = matrix.shape[0]
    cols = panel.shape[0]
    tile = tile_rows(rows)
    piece = pl.BlockSpec((tile, NB), lambda i: (i, 0))
    return pl.pallas_call(
        product_kernel,
        grid=(rows // tile,),
        in_specs=[
            pl.BlockSpec((tile, cols), lambda i: (i, index)),
            pl.BlockSpec((cols, NB), lambda i: (0, 0)),
            *[piece for _ in before],
        ],
        out_specs=piece,
        out_shape=jax.ShapeDtypeStruct((rows, NB), F32),
        scratch_shapes=[pltpu.VMEM((cols, 2 * NB), BF16)],
        compiler_params=pltpu.CompilerParams(vmem_limit_bytes=40 * 1024 * 1024),
        cost_estimate=pl.CostEstimate(
            flops=8 * rows * cols * NB, bytes_accessed=4 * rows * cols, transcendentals=0
        ),
        name="product",
    )(matrix, panel, *before)


def subtract_kernel(a_ref, left_w, left_y, right_w, right_y, *refs):
    out_ref, right = refs[-2:]

    @pl.when(pl.program_id(0) == 0)
    def _():
        for place, ref in ((0, right_w), (3, right_y)):
            high, low = halves(ref[...])
            right[:, place * NB : (place + 1) * NB] = high
            right[:, (place + 1) * NB : (place + 2) * NB] = low
            right[:, (place + 2) * NB : (place + 3) * NB] = high

    parts = []
    for ref in (left_w, left_y):
        high, low = halves(ref[...])
        parts += [high, high, low]
    left = jnp.concatenate(parts, axis=1)
    cols = a_ref.shape[1]
    step = 512 if cols % 512 == 0 else cols
    for first in range(0, cols, step):
        part = lax.dot_general(
            left, right[first : first + step, :], (((1,), (1,)), ((), ())), preferred_element_type=F32
        )
        out_ref[:, first : first + step] = a_ref[:, first : first + step] - part


def subtract(matrix, index, left, right, out_cols, out_index, into=()):
    rows = matrix.shape[0]
    cols = right[0].shape[0]
    tile = tile_rows(rows)
    return pl.pallas_call(
        subtract_kernel,
        grid=(rows // tile,),
        in_specs=[
            pl.BlockSpec((tile, cols), lambda i: (i, index)),
            *[pl.BlockSpec((tile, NB), lambda i: (i, 0))] * 2,
            *[pl.BlockSpec((cols, NB), lambda i: (0, 0))] * 2,
            *[pl.BlockSpec(memory_space=pl.ANY) for _ in into],
        ],
        out_specs=pl.BlockSpec((tile, cols), lambda i: (i, out_index)),
        out_shape=jax.ShapeDtypeStruct((rows, out_cols), F32),
        scratch_shapes=[pltpu.VMEM((cols, 6 * NB), BF16)],
        input_output_aliases={5: 0} if into else {},
        compiler_params=pltpu.CompilerParams(vmem_limit_bytes=48 * 1024 * 1024),
        cost_estimate=pl.CostEstimate(
            flops=12 * rows * cols * NB, bytes_accessed=8 * rows * cols, transcendentals=0
        ),
        name="subtract",
    )(matrix, *left, *right, *into)


def factor_kernel(gram_ref, out_ref, rest, side):
    rest[...] = gram_ref[...]
    down = lax.broadcasted_iota(jnp.int32, (NB, NB), 0)
    side[...] = jnp.where(down == lax.broadcasted_iota(jnp.int32, (NB, NB), 1), 1.0, 0.0)
    for first in range(0, NB, GROUP):
        end = first + GROUP
        rows = [rest[i : i + 1, :] for i in range(first, end)]
        sides = [side[i : i + 1, :] for i in range(first, end)]
        corner = {
            (i, j): jnp.broadcast_to(rows[i][:, first + j : first + j + 1], (1, NB))
            for i in range(GROUP)
            for j in range(i + 1)
        }
        for j in range(GROUP):
            pivot = corner[j, j]
            scale = lax.rsqrt(pivot)
            scale = scale * (1.5 - 0.5 * pivot * scale * scale)
            rows[j] = rows[j] * scale
            sides[j] = sides[j] * scale
            low = {i: corner[i, j] * scale for i in range(j + 1, GROUP)}
            for i in range(j + 1, GROUP):
                rows[i] = rows[i] - low[i] * rows[j]
                sides[i] = sides[i] - low[i] * sides[j]
                for k in range(j + 1, i + 1):
                    corner[i, k] = corner[i, k] - low[i] * low[k]
        upper = jnp.concatenate(rows, axis=0)
        inverse = jnp.concatenate(sides, axis=0)
        side[first:end, :] = inverse
        if end < NB:
            taken = contract(upper, jnp.concatenate([upper, inverse], axis=1), 0, 0)
            rest[end:, :] = rest[end:, :] - taken[end:, :NB]
            side[end:, :] = side[end:, :] - taken[end:, NB:]
    out_ref[...] = side[...].T


def inverse_factor(gram):
    return pl.pallas_call(
        factor_kernel,
        out_shape=jax.ShapeDtypeStruct((NB, NB), F32),
        scratch_shapes=[pltpu.VMEM((NB, NB), F32)] * 2,
        compiler_params=pltpu.CompilerParams(vmem_limit_bytes=16 * 1024 * 1024),
        cost_estimate=pl.CostEstimate(flops=4 * NB**3, bytes_accessed=8 * NB * NB, transcendentals=NB),
        name="factor",
    )(gram)


def after(value, *others):
    return value + jnp.float32(0.0) * sum(other[0, 0] for other in others)


class Grid:
    def __init__(self):
        self.rows = lax.axis_size("row")
        self.cols = lax.axis_size("col")
        self.row = lax.axis_index("row")
        self.col = lax.axis_index("col")
        self.width = self.cols // CORES
        self.depth = self.rows // self.width
        self.sources = self.rows // self.cols
        self.z = self.row // self.width
        self.x = self.row % self.width

    def device(self, z, x, col):
        return (z * self.width + x) * self.cols + col

    def send(self, value, pairs):
        return lax.ppermute(value, AXES, pairs)

    def swap(self, value, axis, bit):
        size = lax.axis_size(axis)
        return lax.ppermute(value, axis, [(i, i ^ bit) for i in range(size)])

    def add_over(self, value, axis, bit):
        while bit < lax.axis_size(axis):
            value = value + self.swap(value, axis, bit)
            bit *= 2
        return value

    def join_cores(self, half):
        other = self.swap(half, "col", 1)
        first = self.col % CORES == 0
        return jnp.concatenate([jnp.where(first, half, other), jnp.where(first, other, half)], axis=0)

    def own_half(self, value):
        half = value.shape[0] // CORES
        return lax.dynamic_slice_in_dim(value, self.col % CORES * half, half, axis=0)

    def other_half(self, value):
        half = value.shape[0] // CORES
        return lax.dynamic_slice_in_dim(value, (1 - self.col % CORES) * half, half, axis=0)

    def sum_half(self, value):
        mine = self.own_half(value) + self.swap(self.other_half(value), "col", 1)
        return self.add_over(mine, "col", CORES)

    def from_chip_zero(self, value):
        half = self.own_half(value)
        total = jnp.where(self.col < CORES, half, jnp.zeros_like(half))
        for y in range(1, self.cols // CORES):
            pairs = [
                (r * self.cols + core, r * self.cols + y * CORES + core)
                for r in range(self.rows)
                for core in range(CORES)
            ]
            total = total + self.send(half, pairs)
        return self.join_cores(total)

    def to_columns(self, item, chunks):
        size = item.shape[0] // chunks
        return zip(*[self.gather(item[i * size : (i + 1) * size]) for i in range(chunks)])

    def gather(self, item):
        wide, deep, cols, count = self.width, self.depth, self.cols, self.sources

        def pairs(moves):
            found = []
            for col in range(cols):
                mirror = col // wide == 1
                for m, n in moves:
                    z, to = (deep - 1 - m, deep - 1 - n) if mirror else (m, n)
                    found.append((self.device(z, col % wide, col), self.device(to, col % wide, col)))
            return found

        mirror = self.col // wide == 1
        place = jnp.where(mirror, deep - 1 - self.z, self.z)
        home = self.x == self.col % wide
        even = range(0, deep, 2)
        near = self.send(item, pairs([(e, e + 1) for e in even]))
        far = {
            t: self.send(item, pairs([(e, (e + 2 * t) % deep) for e in even])) for t in range(1, count)
        }
        down = {}
        for d in range(count - 1):
            value = item if d == 0 else far[count - d]
            down[d] = self.send(value, pairs([(e, e - 1) for e in even if e >= 2 and e + 2 * d < deep]))
        up = {t: self.send(far[t], pairs([(e, e + 1) for e in even if e >= 2 * t])) for t in far}
        relative = [jnp.where(place % 2 == 0, item, near)]
        for t in range(1, count):
            relative.append(far[t] + up[t] + down[count - 1 - t])
        whole = []
        for value in relative:
            crossed = jnp.zeros_like(value)
            for d in range(1, wide):
                moves = [
                    (self.device(z, col % wide, col), self.device(z, (col + d) % wide, col))
                    for z in range(deep)
                    for col in range(cols)
                ]
                crossed = crossed + self.send(value, moves)
            whole.append(jnp.where(home, value, crossed))
        own = self.z // 2
        slots = []
        for j in range(count):
            t = jnp.where(mirror, j - own, own - j) % count
            slots.append(lax.select_n(t, *whole) if count > 2 else jnp.where(t == 0, whole[0], whole[1]))
        shaped = [s.reshape(-1, 1, NB, s.shape[1]) for s in slots]
        return jnp.concatenate(shaped, axis=1).reshape(-1, item.shape[1]), near, relative[1]


def body(matrix):
    grid = Grid()
    local_rows, local_cols = matrix.shape
    chunks = 2
    width = local_cols // chunks
    row_slot = jnp.arange(local_rows, dtype=jnp.int32)
    col_slot = jnp.arange(local_cols, dtype=jnp.int32)
    natural_rows = ((row_slot // NB * grid.rows + grid.row) * NB + row_slot % NB)[:, None]
    natural_cols = ((col_slot // NB * grid.cols + grid.col) * NB + col_slot % NB)[:, None]
    zero = jnp.float32(0.0)

    def below(value, natural, panel):
        return jnp.where(natural >= (panel + 1) * NB, value, zero)

    def block_one(value):
        return jnp.where(grid.row == 1, value[:NB], zero)

    mine = matrix[:, :NB]
    other = grid.swap(mine, "col", 1)
    first = grid.col % CORES == 0
    p0 = below(grid.from_chip_zero(jnp.where(first, mine, other)), natural_rows, 0)
    p0c, early, late = grid.to_columns(p0, chunks)

    b1 = grid.from_chip_zero(after(jnp.where(first, other, mine), early[0]))
    (b1c,), _, b1_late = grid.to_columns(after(b1, late[-1]), 1)

    y0 = ()
    for i in range(chunks):
        y0 = (product(matrix, p0c[i], i, y0),)
        if i == 0:
            small = jnp.concatenate([contract(p0, p0, 0, 0), block_one(p0)], axis=0)
            small = grid.add_over(after(small, y0[0]), "row", 1)
    half = grid.sum_half(y0[0])
    y0 = grid.join_cores(after(half, b1_late[0]))
    y0c, early, late = grid.to_columns(y0, chunks)
    t0 = inverse_factor(small[:NB])
    p0_one = small[NB:]
    w0 = contract(p0, t0, 1, 0)
    w0c = [contract(part, t0, 1, 0) for part in p0c]
    w0_one = contract(p0_one, t0, 1, 0)
    small = grid.add_over(jnp.concatenate([contract(w0, y0, 0, 0), block_one(y0)], axis=0), "row", 1)
    m0, y0_one = contract(small[:NB], t0, 1, 0), small[NB:]

    def coupled(m, t, w, y):
        return 2.0 * contract(t, y, 0, 0) - 4.0 * contract(m, w, 1, 0), 2.0 * contract(t, w, 1, 0)

    def lefts(m, t, w, y):
        return 2.0 * contract(y, t, 1, 0) - 4.0 * contract(w, m, 1, 0), 2.0 * contract(w, t, 1, 1)

    for_w, for_y = coupled(m0, t0, w0_one.T, y0_one.T)
    p1 = below(b1 - contract(w0, for_w, 1, 0) - contract(y0, for_y, 1, 0), natural_rows, 1)
    p1c = []
    y1 = ()
    for i in range(chunks):
        here = slice(i * width, (i + 1) * width)
        part = b1c[here] - contract(w0c[i], for_w, 1, 0) - contract(y0c[i], for_y, 1, 0)
        p1c.append(below(part, natural_cols[here], 1))
        y1 = (product(matrix, p1c[i], i, y1),)
        if i == 0:
            small = jnp.concatenate([contract(side, p1, 0, 0) for side in (w0, y0, p1)], axis=0)
            small = grid.add_over(after(small, p1c[0]), "row", 1)
    t1 = inverse_factor(after(small[2 * NB :], y1[0]))
    for_w, for_y = coupled(m0, t0, small[:NB], small[NB : 2 * NB])
    half = grid.sum_half(y1[0])
    half = half - contract(grid.own_half(w0), for_w, 1, 0) - contract(grid.own_half(y0), for_y, 1, 0)
    y1 = grid.join_cores(half)
    y1c, early, late = grid.to_columns(y1, chunks)
    w1 = contract(p1, t1, 1, 0)
    w1c = [contract(part, t1, 1, 0) for part in p1c]
    m1 = contract(grid.add_over(contract(w1, y1, 0, 0), "row", 1), t1, 1, 0)

    left = lefts(m0, t0, w0, y0)
    middle = []
    for i in range(chunks):
        held = (after(left[0], (early + late)[i]), left[1])
        middle.append(subtract(matrix, i, held, (w0c[i], y0c[i]), width, 0))
    left = lefts(m1, t1, w1, y1)
    updated = ()
    for i in range(chunks):
        updated = (subtract(middle[i], 0, left, (w1c[i], y1c[i]), local_cols, i, updated),)
    return updated[0]


def solution(mesh):
    placed = (P("row", "col"),)
    return jax.shard_map(
        body, mesh=mesh, in_specs=placed, out_specs=P("row", "col"), check_vma=False
    )
```

profile of v0, /device:TPU:4, one launch (start us, length us, event | category | flops | bytes accessed | tf_op | source)
XLA Modules:
  0.0 396.4 jit_solution(13820113145654948887)
XLA Ops:
  5.4 14.7 %collective-permute-done.1 = f32[1024,128]{1,0:T(8,128)} collective-permute-done((f32[1024,128]{1,0:T(8,128)S(1)}, f32[1024,128]{1,0:T(8,128)}, u32[]{:S(2)}, u32[]{:S(2)}) %collective-permute-start.1) | collective-permute-done | bytes 524320 | tf_op jit(solution)/shard_map/ppermute | solution.py:187
  27.2 8.6 %collective-permute-done.3 = f32[1024,128]{1,0:T(8,128)} collective-permute-done((f32[1024,128]{1,0:T(8,128)}, f32[1024,128]{1,0:T(8,128)}, u32[]{:S(2)}, u32[]{:S(2)}) %collective-permute-start.3) | collective-permute-done | bytes 524320 | tf_op jit(solution)/shard_map/ppermute | solution.py:187
  44.4 4.6 %collective-permute-done.9 = f32[1024,128]{1,0:T(8,128)S(1)} collective-permute-done((f32[1024,128]{1,0:T(8,128)}, f32[1024,128]{1,0:T(8,128)S(1)}, u32[]{:S(2)}, u32[]{:S(2)}) %collective-permute-start.9) | collective-permute-done | bytes 524320 | tf_op jit(solution)/shard_map/ppermute | solution.py:187
  71.8 5.6 %collective-permute-done.14 = f32[1024,128]{1,0:T(8,128)S(1)} collective-permute-done((f32[1024,128]{1,0:T(8,128)S(1)}, f32[1024,128]{1,0:T(8,128)S(1)}, u32[]{:S(2)}, u32[]{:S(2)}) %collective-permute-start.14) | collective-permute-done | bytes 524320 | tf_op jit(solution)/shard_map/ppermute | solution.py:187
  77.7 8.6 %product.4.refs_0_ = f32[2048,128]{1,0:T(8,128)S(1)} custom-call(f32[2048,4096]{1,0:T(8,128)} %a_ref.11, f32[2048,128]{1,0:T(8,128)S(1)} %bitcast.101), custom_call_target="tpu_custom_call" | custom-call | flops 4294967296 | bytes 16777216 | tf_op jit(solution)/shard_map/product/pallas_call | solution.py:52
  96.6 8.6 %product.5 = f32[2048,128]{1,0:T(8,128)S(1)} custom-call(f32[2048,4096]{1,0:T(8,128)} %a_ref.11, f32[2048,128]{1,0:T(8,128)S(1)} %bitcast.103, f32[2048,128]{1,0:T(8,128)S(1)} %product.4.refs_0_), custom_call_target="tpu_custom_call" | custom-call | flops 4294967296 | bytes 16777216 | tf_op jit(solution)/shard_map/product/pallas_call | solution.py:52
  108.0 7.1 %collective-permute-done.25 = f32[256,128]{1,0:T(8,128)S(1)} collective-permute-done((f32[256,128]{1,0:T(8,128)S(1)}, f32[256,128]{1,0:T(8,128)S(1)}, u32[]{:S(2)}, u32[]{:S(2)}) %collective-permute-start.25) | collective-permute-done | bytes 131104 | tf_op jit(solution)/shard_map/ppermute | solution.py:191
  115.2 8.4 %factor.2 = f32[128,128]{1,0:T(8,128)S(1)} custom-call(f32[128,128]{1,0:T(8,128)S(1)} %slice.113.gram_ref), custom_call_target="tpu_custom_call" | custom-call | flops 8388608 | bytes 131072 | tf_op jit(solution)/shard_map/factor/pallas_call | solution.py:157
  126.4 11.8 %collective-permute-done.16 = f32[1024,128]{1,0:T(8,128)S(1)} collective-permute-done((f32[1024,128]{1,0:T(8,128)S(1)}, f32[1024,128]{1,0:T(8,128)S(1)}, u32[]{:S(2)}, u32[]{:S(2)}) %collective-permute-start.16) | collective-permute-done | bytes 524320 | tf_op jit(solution)/shard_map/ppermute | solution.py:191
  153.8 12.9 %collective-permute-start.34 = (f32[1024,128]{1,0:T(8,128)S(1)}, f32[1024,128]{1,0:T(8,128)S(1)}, u32[]{:S(2)}, u32[]{:S(2)}) collective-permute-start(f32[1024,128]{1,0:T(8,128)S(1)} %get-tuple-element.25), channel_id=1, source_target_pairs={{0,16},{16,0},{5,21},{21,5},{26,10},{10,26},{31,15},{15,31}} | collective-permute-start | bytes 1572872 | tf_op jit(solution)/shard_map/ppermute | solution.py:187
  188.8 11.3 %collective-permute-done.38 = f32[1024,128]{1,0:T(8,128)S(1)} collective-permute-done((f32[1024,128]{1,0:T(8,128)S(1)}, f32[1024,128]{1,0:T(8,128)S(1)}, u32[]{:S(2)}, u32[]{:S(2)}) %collective-permute-start.38) | collective-permute-done | bytes 524320 | tf_op jit(solution)/shard_map/ppermute | solution.py:187
  205.1 6.1 %collective-permute-done.41 = f32[1024,128]{1,0:T(8,128)S(1)} collective-permute-done((f32[1024,128]{1,0:T(8,128)S(1)}, f32[1024,128]{1,0:T(8,128)S(1)}, u32[]{:S(2)}, u32[]{:S(2)}) %collective-permute-start.41) | collective-permute-done | bytes 524320 | tf_op jit(solution)/shard_map/ppermute | solution.py:187
  221.6 8.6 %product.6.refs_0_ = f32[2048,128]{1,0:T(8,128)S(1)} custom-call(f32[2048,4096]{1,0:T(8,128)} %a_ref.11, f32[2048,128]{1,0:T(8,128)S(1)} %fusion.3.p_ref), custom_call_target="tpu_custom_call" | custom-call | flops 4294967296 | bytes 16777216 | tf_op jit(solution)/shard_map/product/pallas_call | solution.py:52
  231.4 9.0 %product.7 = f32[2048,128]{1,0:T(8,128)S(1)} custom-call(f32[2048,4096]{1,0:T(8,128)} %a_ref.11, f32[2048,128]{1,0:T(8,128)S(1)} %fusion.4.p_ref, f32[2048,128]{1,0:T(8,128)S(1)} %product.6.refs_0_), custom_call_target="tpu_custom_call" | custom-call | flops 4294967296 | bytes 16777216 | tf_op jit(solution)/shard_map/product/pallas_call | solution.py:52
  243.2 5.6 %collective-permute-done.46 = f32[384,128]{1,0:T(8,128)S(1)} collective-permute-done((f32[384,128]{1,0:T(8,128)S(1)}, f32[384,128]{1,0:T(8,128)S(1)}, u32[]{:S(2)}, u32[]{:S(2)}) %collective-permute-start.46) | collective-permute-done | bytes 196640 | tf_op jit(solution)/shard_map/ppermute | solution.py:191
  249.8 5.7 %collective-permute-done.47 = f32[384,128]{1,0:T(8,128)S(1)} collective-permute-done((f32[384,128]{1,0:T(8,128)S(1)}, f32[384,128]{1,0:T(8,128)S(1)}, u32[]{:S(2)}, u32[]{:S(2)}) %collective-permute-start.47) | collective-permute-done | bytes 196640 | tf_op jit(solution)/shard_map/ppermute | solution.py:191
  257.6 9.0 %collective-permute-done.48 = f32[384,128]{1,0:T(8,128)S(1)} collective-permute-done((f32[384,128]{1,0:T(8,128)S(1)}, f32[384,128]{1,0:T(8,128)S(1)}, u32[]{:S(2)}, u32[]{:S(2)}) %collective-permute-start.48) | collective-permute-done | bytes 196640 | tf_op jit(solution)/shard_map/ppermute | solution.py:191
  271.8 8.4 %factor.3 = f32[128,128]{1,0:T(8,128)S(1)} custom-call(f32[128,128]{1,0:T(8,128)S(1)} %slice_add_fusion.gram_ref), custom_call_target="tpu_custom_call" | custom-call | flops 8388608 | bytes 131072 | tf_op jit(solution)/shard_map/factor/pallas_call | solution.py:157
  302.4 6.5 %collective-permute-done.59 = f32[1024,128]{1,0:T(8,128)S(1)} collective-permute-done((f32[1024,128]{1,0:T(8,128)S(1)}, f32[1024,128]{1,0:T(8,128)S(1)}, u32[]{:S(2)}, u32[]{:S(2)}) %collective-permute-start.59) | collective-permute-done | bytes 524320 | tf_op jit(solution)/shard_map/ppermute | solution.py:187
  319.3 15.3 %subtract.5.a_ref = f32[2048,2048]{1,0:T(8,128)} custom-call(f32[2048,4096]{1,0:T(8,128)} %a_ref.11, f32[2048,128]{1,0:T(8,128)S(1)} %get-tuple-element.21.left_w, f32[2048,128]{1,0:T(8,128)S(1)} %convolution_multiply_fusion.3.left_y, f32[2048,128]{1,0:T(8,128)S(1)} %fusion.66.right_w, f32[2048,128]{1,0:T(8,128)S(1)} %bitcast.108), custom_call_target="tpu_custom_call" | custom-call | flops 6442450944 | bytes 33554432 | tf_op jit(solution)/shard_map/subtract/pallas_call | solution.py:100
  339.8 8.4 %collective-permute-done.56 = f32[1024,128]{1,0:T(8,128)S(1)} collective-permute-done((f32[1024,128]{1,0:T(8,128)S(1)}, f32[1024,128]{1,0:T(8,128)S(1)}, u32[]{:S(2)}, u32[]{:S(2)}) %collective-permute-start.56) | collective-permute-done | bytes 524320 | tf_op jit(solution)/shard_map/ppermute | solution.py:187
  349.6 15.5 %subtract.4.a_ref = f32[2048,2048]{1,0:T(8,128)} custom-call(f32[2048,4096]{1,0:T(8,128)} %a_ref.11, f32[2048,128]{1,0:T(8,128)S(1)} %get-tuple-element.22.left_w, f32[2048,128]{1,0:T(8,128)S(1)} %convolution_multiply_fusion.3.left_y, f32[2048,128]{1,0:T(8,128)S(1)} %fusion.65.right_w, f32[2048,128]{1,0:T(8,128)S(1)} %bitcast.106), custom_call_target="tpu_custom_call" | custom-call | flops 6442450944 | bytes 33554432 | tf_op jit(solution)/shard_map/subtract/pallas_call | solution.py:100
  365.5 15.3 %subtract.6.refs_0_ = f32[2048,4096]{1,0:T(8,128)} custom-call(f32[2048,2048]{1,0:T(8,128)} %subtract.5.a_ref, f32[2048,128]{1,0:T(8,128)S(1)} %fusion.left_w, f32[2048,128]{1,0:T(8,128)S(1)} %convolution_multiply_fusion.left_y, f32[2048,128]{1,0:T(8,128)S(1)} %fusion.71.right_w, f32[2048,128]{1,0:T(8,128)S(1)} %bitcast.110), custom_call_target="tpu_custom_call" | custom-call | flops 6442450944 | bytes 33554432 | tf_op jit(solution)/shard_map/subtract/pallas_call | solution.py:100
  380.9 15.3 %subtract.7 = f32[2048,4096]{1,0:T(8,128)} custom-call(f32[2048,2048]{1,0:T(8,128)} %subtract.4.a_ref, f32[2048,128]{1,0:T(8,128)S(1)} %fusion.left_w, f32[2048,128]{1,0:T(8,128)S(1)} %convolution_multiply_fusion.left_y, f32[2048,128]{1,0:T(8,128)S(1)} %fusion.70.right_w, f32[2048,128]{1,0:T(8,128)S(1)} %bitcast.109, ...), custom_call_target="tpu_custom_call", output_to_operand_aliasing={{}: (5, {})} | custom-call | flops 6442450944 | bytes 33554432 | tf_op jit(solution)/shard_map/subtract/pallas_call | solution.py:100
  (232 shorter events, 158.6 us)
Async XLA Ops:
  43.7 21.3 %collective-permute-start.13 = (f32[1024,128]{1,0:T(8,128)}, f32[1024,128]{1,0:T(8,128)S(1)}, u32[]{:S(2)}, u32[]{:S(2)}) collective-permute-start(f32[1024,128]{1,0:T(8,128)} %get-tuple-element.30), channel_id=1, source_target_pairs={{16,8},{21,13},{10,18},{15,23}} | collective-permute-start | bytes 1572872 | tf_op jit(solution)/shard_map/ppermute | solution.py:187
  49.0 21.7 %collective-permute-start.4 = (f32[1024,128]{1,0:T(8,128)S(1)}, f32[1024,128]{1,0:T(8,128)S(1)}, u32[]{:S(2)}, u32[]{:S(2)}) collective-permute-start(f32[1024,128]{1,0:T(8,128)S(1)} %get-tuple-element.29), channel_id=1, source_target_pairs={{0,4},{5,1},{2,6},{7,3},{8,12},{13,9},{10,14},{15,11},{16,20},{21,... | collective-permute-start | bytes 1572872 | tf_op jit(solution)/shard_map/ppermute | solution.py:187
  71.1 24.2 %collective-permute-start.19 = (f32[2048,128]{1,0:T(8,128)S(1)}, f32[2048,128]{1,0:T(8,128)S(1)}, u32[]{:S(2)}, u32[]{:S(2)}) collective-permute-start(f32[2048,128]{1,0:T(8,128)S(1)} %fusion.10), channel_id=1, source_target_pairs={{0,16},{16,0},{5,21},{21,5},{26,10},{10,26},{31,15},{15,31}} | collective-permute-start | bytes 3145736 | tf_op jit(solution)/shard_map/ppermute | solution.py:187
  90.2 34.9 %collective-permute-start.21 = (f32[2048,128]{1,0:T(8,128)S(1)}, f32[2048,128]{1,0:T(8,128)S(1)}, u32[]{:S(2)}, u32[]{:S(2)}) collective-permute-start(f32[2048,128]{1,0:T(8,128)S(1)} %fusion.10), channel_id=1, source_target_pairs={{16,8},{21,13},{10,18},{15,23}} | collective-permute-start | bytes 3145736 | tf_op jit(solution)/shard_map/ppermute | solution.py:187
  95.3 29.8 %collective-permute-start.20 = (f32[2048,128]{1,0:T(8,128)S(1)}, f32[2048,128]{1,0:T(8,128)S(1)}, u32[]{:S(2)}, u32[]{:S(2)}) collective-permute-start(f32[2048,128]{1,0:T(8,128)S(1)} %collective-permute-done.19), channel_id=1, source_target_pairs={{16,24},{21,29},{10,2},{15,7}} | collective-permute-start | bytes 3145736 | tf_op jit(solution)/shard_map/ppermute | solution.py:187
  105.2 19.4 %collective-permute-start.15 = (f32[1024,128]{1,0:T(8,128)S(1)}, f32[1024,128]{1,0:T(8,128)S(1)}, u32[]{:S(2)}, u32[]{:S(2)}) collective-permute-start(f32[1024,128]{1,0:T(8,128)S(1)} %constant_dynamic-slice_fusion.1), channel_id=1, source_target_pairs={{0,1},{1,0},{2,3},{3,2},{4,5},{5,4},{6,7},{7,6},{8,9},{9,8},{10,11... | collective-permute-start | bytes 1572872 | tf_op jit(solution)/shard_map/ppermute | solution.py:191
  106.5 42.1 %collective-permute-start.29 = (f32[2048,128]{1,0:T(8,128)S(1)}, f32[2048,128]{1,0:T(8,128)S(1)}, u32[]{:S(2)}, u32[]{:S(2)}) collective-permute-start(f32[2048,128]{1,0:T(8,128)S(1)} %fusion.10), channel_id=1, source_target_pairs={{0,8},{16,24},{5,13},{21,29},{26,18},{10,2},{31,23},{15,7}} | collective-permute-start | bytes 3145736 | tf_op jit(solution)/shard_map/ppermute | solution.py:187
  148.4 18.3 %collective-permute-start.27 = (f32[256,128]{1,0:T(8,128)S(1)}, f32[256,128]{1,0:T(8,128)S(1)}, u32[]{:S(2)}, u32[]{:S(2)}) collective-permute-start(f32[256,128]{1,0:T(8,128)S(1)} %fusion.62), channel_id=1, source_target_pairs={{0,8},{4,12},{8,0},{12,4},{16,24},{20,28},{24,16},{28,20},{1,9},{5... | collective-permute-start | bytes 393224 | tf_op jit(solution)/shard_map/ppermute | solution.py:191
  148.6 33.6 %collective-permute-start.30 = (f32[2048,128]{1,0:T(8,128)S(1)}, f32[2048,128]{1,0:T(8,128)S(1)}, u32[]{:S(2)}, u32[]{:S(2)}) collective-permute-start(f32[2048,128]{1,0:T(8,128)S(1)} %broadcast_select_fusion.1), channel_id=1, source_target_pairs={{0,4},{5,1},{2,6},{7,3},{8,12},{13,9},{10,14},{15,11},{16,20},{21,... | collective-permute-start | bytes 3145736 | tf_op jit(solution)/shard_map/ppermute | solution.py:187
  151.7 31.3 %collective-permute-start.31 = (f32[2048,128]{1,0:T(8,128)S(1)}, f32[2048,128]{1,0:T(8,128)S(1)}, u32[]{:S(2)}, u32[]{:S(2)}) collective-permute-start(f32[2048,128]{1,0:T(8,128)S(1)} %add_add_fusion), channel_id=1, source_target_pairs={{0,4},{5,1},{2,6},{7,3},{8,12},{13,9},{10,14},{15,11},{16,20},{21,... | collective-permute-start | bytes 3145736 | tf_op jit(solution)/shard_map/ppermute | solution.py:187
  153.1 60.5 %collective-permute-start.36 = (f32[1024,128]{1,0:T(8,128)S(1)}, f32[1024,128]{1,0:T(8,128)S(1)}, u32[]{:S(2)}, u32[]{:S(2)}) collective-permute-start(f32[1024,128]{1,0:T(8,128)S(1)} %get-tuple-element.25), channel_id=1, source_target_pairs={{16,8},{21,13},{10,18},{15,23}} | collective-permute-start | bytes 1572872 | tf_op jit(solution)/shard_map/ppermute | solution.py:187
  153.8 48.6 %collective-permute-start.34 = (f32[1024,128]{1,0:T(8,128)S(1)}, f32[1024,128]{1,0:T(8,128)S(1)}, u32[]{:S(2)}, u32[]{:S(2)}) collective-permute-start(f32[1024,128]{1,0:T(8,128)S(1)} %get-tuple-element.25), channel_id=1, source_target_pairs={{0,16},{16,0},{5,21},{21,5},{26,10},{10,26},{31,15},{15,31}} | collective-permute-start | bytes 1572872 | tf_op jit(solution)/shard_map/ppermute | solution.py:187
  183.0 17.1 %collective-permute-start.38 = (f32[1024,128]{1,0:T(8,128)S(1)}, f32[1024,128]{1,0:T(8,128)S(1)}, u32[]{:S(2)}, u32[]{:S(2)}) collective-permute-start(f32[1024,128]{1,0:T(8,128)S(1)} %get-tuple-element.26), channel_id=1, source_target_pairs={{0,8},{16,24},{5,13},{21,29},{26,18},{10,2},{31,23},{15,7}} | collective-permute-start | bytes 1572872 | tf_op jit(solution)/shard_map/ppermute | solution.py:187
  186.7 17.1 %collective-permute-start.42 = (f32[1024,128]{1,0:T(8,128)S(1)}, f32[1024,128]{1,0:T(8,128)S(1)}, u32[]{:S(2)}, u32[]{:S(2)}) collective-permute-start(f32[1024,128]{1,0:T(8,128)S(1)} %get-tuple-element.26), channel_id=1, source_target_pairs={{16,8},{21,13},{10,18},{15,23}} | collective-permute-start | bytes 1572872 | tf_op jit(solution)/shard_map/ppermute | solution.py:187
  187.4 42.8 %collective-permute-start.33 = (f32[1024,128]{1,0:T(8,128)S(1)}, f32[1024,128]{1,0:T(8,128)S(1)}, u32[]{:S(2)}, u32[]{:S(2)}) collective-permute-start(f32[1024,128]{1,0:T(8,128)S(1)} %broadcast_select_fusion.14), channel_id=1, source_target_pairs={{0,4},{5,1},{2,6},{7,3},{8,12},{13,9},{10,14},{15,11},{16,20},{21,... | collective-permute-start | bytes 1572872 | tf_op jit(solution)/shard_map/ppermute | solution.py:187
  295.5 40.4 %collective-permute-start.63 = (f32[1024,128]{1,0:T(8,128)S(1)}, f32[1024,128]{1,0:T(8,128)S(1)}, u32[]{:S(2)}, u32[]{:S(2)}) collective-permute-start(f32[1024,128]{1,0:T(8,128)S(1)} %get-tuple-element.23), channel_id=1, source_target_pairs={{16,8},{21,13},{10,18},{15,23}} | collective-permute-start | bytes 1572872 | tf_op jit(solution)/shard_map/ppermute | solution.py:187
  296.2 21.8 %collective-permute-start.61 = (f32[1024,128]{1,0:T(8,128)S(1)}, f32[1024,128]{1,0:T(8,128)S(1)}, u32[]{:S(2)}, u32[]{:S(2)}) collective-permute-start(f32[1024,128]{1,0:T(8,128)S(1)} %get-tuple-element.23), channel_id=1, source_target_pairs={{0,16},{16,0},{5,21},{21,5},{26,10},{10,26},{31,15},{15,31}} | collective-permute-start | bytes 1572872 | tf_op jit(solution)/shard_map/ppermute | solution.py:187
  298.2 41.5 %collective-permute-start.57 = (f32[1024,128]{1,0:T(8,128)S(1)}, f32[1024,128]{1,0:T(8,128)S(1)}, u32[]{:S(2)}, u32[]{:S(2)}) collective-permute-start(f32[1024,128]{1,0:T(8,128)S(1)} %get-tuple-element.24), channel_id=1, source_target_pairs={{16,8},{21,13},{10,18},{15,23}} | collective-permute-start | bytes 1572872 | tf_op jit(solution)/shard_map/ppermute | solution.py:187
  308.9 25.7 %collective-permute-start.55 = (f32[1024,128]{1,0:T(8,128)S(1)}, f32[1024,128]{1,0:T(8,128)S(1)}, u32[]{:S(2)}, u32[]{:S(2)}) collective-permute-start(f32[1024,128]{1,0:T(8,128)S(1)} %get-tuple-element.24), channel_id=1, source_target_pairs={{0,16},{16,0},{5,21},{21,5},{26,10},{10,26},{31,15},{15,31}} | collective-permute-start | bytes 1572872 | tf_op jit(solution)/shard_map/ppermute | solution.py:187
  314.5 50.5 %collective-permute-start.60 = (f32[1024,128]{1,0:T(8,128)S(1)}, f32[1024,128]{1,0:T(8,128)S(1)}, u32[]{:S(2)}, u32[]{:S(2)}) collective-permute-start(f32[1024,128]{1,0:T(8,128)S(1)} %broadcast_select_fusion.11), channel_id=1, source_target_pairs={{0,4},{5,1},{2,6},{7,3},{8,12},{13,9},{10,14},{15,11},{16,20},{21,... | collective-permute-start | bytes 1572872 | tf_op jit(solution)/shard_map/ppermute | solution.py:187
  318.0 19.3 %collective-permute-start.62 = (f32[1024,128]{1,0:T(8,128)S(1)}, f32[1024,128]{1,0:T(8,128)}, u32[]{:S(2)}, u32[]{:S(2)}) collective-permute-start(f32[1024,128]{1,0:T(8,128)S(1)} %collective-permute-done.61), channel_id=1, source_target_pairs={{16,24},{21,29},{10,2},{15,7}} | collective-permute-start | bytes 1572872 | tf_op jit(solution)/shard_map/ppermute | solution.py:187
  336.0 29.3 %collective-permute-start.54 = (f32[1024,128]{1,0:T(8,128)S(1)}, f32[1024,128]{1,0:T(8,128)S(1)}, u32[]{:S(2)}, u32[]{:S(2)}) collective-permute-start(f32[1024,128]{1,0:T(8,128)S(1)} %broadcast_select_fusion.12), channel_id=1, source_target_pairs={{0,4},{5,1},{2,6},{7,3},{8,12},{13,9},{10,14},{15,11},{16,20},{21,... | collective-permute-start | bytes 1572872 | tf_op jit(solution)/shard_map/ppermute | solution.py:187
  338.4 26.6 %collective-permute-start.64 = (f32[1024,128]{1,0:T(8,128)S(1)}, f32[1024,128]{1,0:T(8,128)S(1)}, u32[]{:S(2)}, u32[]{:S(2)}) collective-permute-start(f32[1024,128]{1,0:T(8,128)S(1)} %add_add_fusion.1), channel_id=1, source_target_pairs={{0,4},{5,1},{2,6},{7,3},{8,12},{13,9},{10,14},{15,11},{16,20},{21,... | collective-permute-start | bytes 1572872 | tf_op jit(solution)/shard_map/ppermute | solution.py:187
  348.2 17.0 %collective-permute-start.58 = (f32[1024,128]{1,0:T(8,128)S(1)}, f32[1024,128]{1,0:T(8,128)S(1)}, u32[]{:S(2)}, u32[]{:S(2)}) collective-permute-start(f32[1024,128]{1,0:T(8,128)S(1)} %add_add_fusion.2), channel_id=1, source_target_pairs={{0,4},{5,1},{2,6},{7,3},{8,12},{13,9},{10,14},{15,11},{16,20},{21,... | collective-permute-start | bytes 1572872 | tf_op jit(solution)/shard_map/ppermute | solution.py:187
  (42 other events, 441.0 us)
where the time goes:
time: 403 us; the launch traced here: 396 us
  waiting for transfers between devices  142 us (35%)
  Pallas kernels  113 us (28%)
  starting transfers between devices  85 us (21%)
  matrix products  32 us (8%)
  other arithmetic  10.3 us (3%)
  between operations  6.82 us (2%)
  local copies, waits for them, and re-layouts  6.7 us (2%)
    ppermute x44, waiting for transfers between devices, send(): return lax.ppermute(value, AXES, pairs)  84.5 us
    ppermute x44, starting transfers between devices, send(): return lax.ppermute(value, AXES, pairs)  63.9 us
    pallas_call x4, Pallas kernels, subtract(): pl.pallas_call(subtract_kernel, grid=(rows // tile,), in_specs=[pl.BlockS...  61.4 us
    ppermute x21, waiting for transfers between devices, swap(): return lax.ppermute(value, axis, [(i, i ^ bit) for i in range(size)])  57.9 us
    pallas_call x4, Pallas kernels, product(): pl.pallas_call(product_kernel, grid=(rows // tile,), in_specs=[pl.BlockSp...  34.9 us
    dot_general x35, matrix products, contract(): lax.dot_general(left, right, (((left_dim,), (right_dim,)), ((), ())), pre...  32 us
    ppermute x21, starting transfers between devices, swap(): return lax.ppermute(value, axis, [(i, i ^ bit) for i in range(size)])  21.1 us
    pallas_call x2, Pallas kernels, inverse_factor(): pl.pallas_call(factor_kernel, out_shape=jax.ShapeDtypeStruct((NB, NB), F3...  16.9 us
  transfers between devices with their start and end apart: 65, of which 28 were waited for; matrix products, arithmetic and copies ran while one was open for 10% of the time, Pallas kernels for 19%

commit v1 on v0

v1 whole, which is shorter than its diff:
```python
import functools

import jax
import jax.numpy as jnp
from jax import lax
from jax.experimental import pallas as pl
from jax.experimental.pallas import tpu as pltpu
from jax.sharding import PartitionSpec as P

NB = 128
PANELS = 2
CORES = 2
GROUP = 8
SCALE = 2.0**60
HIGH = lax.Precision.HIGHEST
BF16 = jnp.bfloat16
F32 = jnp.float32
AXES = ("row", "col")


def contract(left, right, left_dim, right_dim):
    return lax.dot_general(left, right, (((left_dim,), (right_dim,)), ((), ())), precision=HIGH)


def tile_rows(rows, most):
    return most if rows % most == 0 else rows


def halves(value):
    high = value.astype(BF16)
    return high, (value - high.astype(F32)).astype(BF16)


def set_panel(ref, both):
    high, low = halves(ref[...])
    both[:, :NB] = high
    both[:, NB:] = low


def set_right(refs, right):
    for place, ref in enumerate(refs):
        high, low = halves(ref[...])
        first = 3 * place * NB
        right[:, first : first + NB] = high
        right[:, first + NB : first + 2 * NB] = low
        right[:, first + 2 * NB : first + 3 * NB] = high


def left_parts(refs):
    parts = []
    for ref in refs:
        high, low = halves(ref[...])
        parts += [high, high, low]
    return jnp.concatenate(parts, axis=1)


def less(a_ref, left, right, first, step):
    part = lax.dot_general(
        left, right[first : first + step, :], (((1,), (1,)), ((), ())), preferred_element_type=F32
    )
    return a_ref[:, first : first + step] - part


def times(a, p):
    high, low = halves(a)
    total = jnp.dot(high, p, preferred_element_type=F32) + jnp.dot(low, p, preferred_element_type=F32)
    return total[:, :NB] + total[:, NB:]


def column_step(cols):
    return 512 if cols % 512 == 0 else cols


def product_kernel(count, a_ref, p_ref, *refs):
    out_ref, both = refs[-2:]

    @pl.when(pl.program_id(0) == 0)
    def _():
        set_panel(p_ref, both)

    total = times(a_ref[...], both[...])
    out_ref[...] = refs[0][...] + total if count else total


def product(matrix, panel, index, before=(), waits=()):
    rows = matrix.shape[0]
    cols = panel.shape[0]
    tile = tile_rows(rows, 512)
    piece = pl.BlockSpec((tile, NB), lambda i: (i, 0))
    return pl.pallas_call(
        functools.partial(product_kernel, len(before)),
        grid=(rows // tile,),
        in_specs=[
            pl.BlockSpec((tile, cols), lambda i: (i, index)),
            pl.BlockSpec((cols, NB), lambda i: (0, 0)),
            *[piece for _ in before],
            *[pl.BlockSpec(memory_space=pl.ANY) for _ in waits],
        ],
        out_specs=piece,
        out_shape=jax.ShapeDtypeStruct((rows, NB), F32),
        scratch_shapes=[pltpu.VMEM((cols, 2 * NB), BF16)],
        compiler_params=pltpu.CompilerParams(vmem_limit_bytes=24 * 1024 * 1024),
        cost_estimate=pl.CostEstimate(
            flops=8 * rows * cols * NB, bytes_accessed=4 * rows * cols, transcendentals=0
        ),
        name="product",
    )(matrix, panel, *before, *waits)


def subtract_kernel(count, a_ref, *refs):
    lefts, rights = refs[:count], refs[count : 2 * count]
    out_ref, right = refs[-2:]

    @pl.when(pl.program_id(0) == 0)
    def _():
        set_right(rights, right)

    left = left_parts(lefts)
    cols = a_ref.shape[1]
    step = column_step(cols)
    for first in range(0, cols, step):
        out_ref[:, first : first + step] = less(a_ref, left, right, first, step)


def subtract(matrix, index, left, right, into=()):
    rows = matrix.shape[0]
    cols = right[0].shape[0]
    count = len(left)
    tile = tile_rows(rows, 256)
    block = pl.BlockSpec((tile, cols), lambda i: (i, index))
    return pl.pallas_call(
        functools.partial(subtract_kernel, count),
        grid=(rows // tile,),
        in_specs=[
            block,
            *[pl.BlockSpec((tile, NB), lambda i: (i, 0))] * count,
            *[pl.BlockSpec((cols, NB), lambda i: (0, 0))] * count,
            *[pl.BlockSpec(memory_space=pl.ANY) for _ in into],
        ],
        out_specs=block,
        out_shape=jax.ShapeDtypeStruct(matrix.shape, F32),
        scratch_shapes=[pltpu.VMEM((cols, 3 * count * NB), BF16)],
        input_output_aliases={2 * count + 1: 0} if into else {},
        compiler_params=pltpu.CompilerParams(vmem_limit_bytes=36 * 1024 * 1024),
        cost_estimate=pl.CostEstimate(
            flops=6 * count * rows * cols * NB, bytes_accessed=8 * rows * cols, transcendentals=0
        ),
        name="subtract",
    )(matrix, *left, *right, *into)


def factor_kernel(gram_ref, *refs):
    out_ref, rest, side = refs[-3:]
    rest[...] = gram_ref[...]
    down = lax.broadcasted_iota(jnp.int32, (NB, NB), 0)
    side[...] = jnp.where(down == lax.broadcasted_iota(jnp.int32, (NB, NB), 1), 1.0, 0.0)
    for first in range(0, NB, GROUP):
        end = first + GROUP
        rows = [rest[i : i + 1, :] for i in range(first, end)]
        sides = [side[i : i + 1, :] for i in range(first, end)]
        corner = {
            (i, j): jnp.broadcast_to(rows[i][:, first + j : first + j + 1], (1, NB))
            for i in range(GROUP)
            for j in range(i + 1)
        }
        for j in range(GROUP):
            pivot = corner[j, j]
            scale = lax.rsqrt(pivot)
            scale = scale * (1.5 - 0.5 * pivot * scale * scale)
            rows[j] = rows[j] * scale
            sides[j] = sides[j] * scale
            low = {i: corner[i, j] * scale for i in range(j + 1, GROUP)}
            for i in range(j + 1, GROUP):
                rows[i] = rows[i] - low[i] * rows[j]
                sides[i] = sides[i] - low[i] * sides[j]
                for k in range(j + 1, i + 1):
                    corner[i, k] = corner[i, k] - low[i] * low[k]
        upper = jnp.concatenate(rows, axis=0)
        inverse = jnp.concatenate(sides, axis=0)
        side[first:end, :] = inverse
        if end < NB:
            taken = contract(upper, jnp.concatenate([upper, inverse], axis=1), 0, 0)
            rest[end:, :] = rest[end:, :] - taken[end:, :NB]
            side[end:, :] = side[end:, :] - taken[end:, NB:]
    out_ref[...] = side[...].T


def inverse_factor(gram, waits=()):
    return pl.pallas_call(
        factor_kernel,
        in_specs=[pl.BlockSpec((NB, NB), lambda: (0, 0)), *[pl.BlockSpec(memory_space=pl.ANY) for _ in waits]],
        out_shape=jax.ShapeDtypeStruct((NB, NB), F32),
        scratch_shapes=[pltpu.VMEM((NB, NB), F32)] * 2,
        compiler_params=pltpu.CompilerParams(vmem_limit_bytes=16 * 1024 * 1024),
        cost_estimate=pl.CostEstimate(flops=4 * NB**3, bytes_accessed=8 * NB * NB, transcendentals=NB),
        name="factor",
    )(gram, *waits)


def after(value, *others):
    return value + jnp.float32(0.0) * sum(other[0, 0] for other in others)


class Grid:
    def __init__(self):
        self.rows = lax.axis_size("row")
        self.cols = lax.axis_size("col")
        self.row = lax.axis_index("row")
        self.col = lax.axis_index("col")
        self.width = self.cols // CORES
        self.depth = self.rows // self.width
        self.sources = self.rows // self.cols
        self.z = self.row // self.width
        self.x = self.row % self.width

    def device(self, z, x, col):
        return (z * self.width + x) * self.cols + col

    def send(self, value, pairs):
        return lax.ppermute(value, AXES, pairs)

    def swap(self, value, axis, bit):
        size = lax.axis_size(axis)
        return lax.ppermute(value, axis, [(i, i ^ bit) for i in range(size)])

    def add_over(self, value, axis, bit):
        while bit < lax.axis_size(axis):
            value = value + self.swap(value, axis, bit)
            bit *= 2
        return value

    def add_all(self, value):
        value = self.add_over(self.add_over(value, "row", 1), "col", CORES)
        return value + self.swap(value, "col", 1)

    def join_cores(self, half):
        other = self.swap(half, "col", 1)
        first = self.col % CORES == 0
        return jnp.concatenate([jnp.where(first, half, other), jnp.where(first, other, half)], axis=0)

    def own_half(self, value):
        half = value.shape[0] // CORES
        return lax.dynamic_slice_in_dim(value, self.col % CORES * half, half, axis=0)

    def other_half(self, value):
        half = value.shape[0] // CORES
        return lax.dynamic_slice_in_dim(value, (1 - self.col % CORES) * half, half, axis=0)

    def sum_half(self, value, *others):
        mine = after(self.own_half(value) + self.swap(self.other_half(value), "col", 1), *others)
        return self.add_over(mine, "col", CORES), mine

    def to_all_chips(self, value):
        total = jnp.where(self.col < CORES, value, jnp.zeros_like(value))
        for pairs in self.from_zero():
            total = total + self.send(value, pairs)
        return total

    def from_zero(self):
        return [
            [
                (r * self.cols + core, r * self.cols + y * CORES + core)
                for r in range(self.rows)
                for core in range(CORES)
            ]
            for y in range(1, self.cols // CORES)
        ]

    def from_chip_zero(self, value, start=(), end=()):
        came = self.to_all_chips(after(self.own_half(value), *start))
        return self.join_cores(after(came, *end)), came

    def to_columns(self, item, chunks):
        size = item.shape[0] // chunks
        found = []
        for i in range(chunks):
            part = item[i * size : (i + 1) * size]
            if found:
                part = after(part, found[-1].first)
            found.append(Gather(self, part, found[-1].crossed if found else ()))
        return found


class Gather:
    def __init__(self, grid, item, before):
        wide, deep, cols, count = grid.width, grid.depth, grid.cols, grid.sources
        self.grid = grid

        def pairs(moves):
            found = []
            for col in range(cols):
                mirror = col // wide == 1
                for m, n in moves:
                    z, to = (deep - 1 - m, deep - 1 - n) if mirror else (m, n)
                    found.append((grid.device(z, col % wide, col), grid.device(to, col % wide, col)))
            return found

        mirror = grid.col // wide == 1
        place = jnp.where(mirror, deep - 1 - grid.z, grid.z)
        even = range(0, deep, 2)
        self.first = grid.send(item, pairs([(e, e + 1) for e in even]))
        far = {t: grid.send(item, pairs([(e, (e + 2 * t) % deep) for e in even])) for t in range(1, count)}
        self.direct = far[1]
        down = {}
        for d in range(count - 1):
            value = item if d == 0 else far[count - d]
            down[d] = grid.send(value, pairs([(e, e - 1) for e in even if e >= 2 and e + 2 * d < deep]))
        up = {t: grid.send(far[t], pairs([(e, e + 1) for e in even if e >= 2 * t])) for t in far}
        self.relative = [jnp.where(place % 2 == 0, item, after(self.first, *before[:1]))]
        self.relative += [far[t] + up[t] + after(down[count - 1 - t], *before[1:]) for t in far]
        self.distant = self.relative[1]
        self.crossed = []
        for value in self.relative:
            crossed = jnp.zeros_like(value)
            for d in range(1, wide):
                moves = [
                    (grid.device(z, col % wide, col), grid.device(z, (col + d) % wide, col))
                    for z in range(deep)
                    for col in range(cols)
                ]
                crossed = crossed + grid.send(value, moves)
            self.crossed.append(crossed)

    def columns(self, *others):
        grid, count = self.grid, self.grid.sources
        home = grid.x == grid.col % grid.width
        whole = [
            jnp.where(home, value, after(crossed, *others))
            for value, crossed in zip(self.relative, self.crossed, strict=True)
        ]
        own = grid.z // 2
        slots = []
        for j in range(count):
            t = jnp.where(grid.col // grid.width == 1, j - own, own - j) % count
            slots.append(lax.select_n(t, *whole) if count > 2 else jnp.where(t == 0, whole[0], whole[1]))
        wide = slots[0].shape[1]
        return jnp.concatenate([s.reshape(-1, 1, NB, wide) for s in slots], axis=1).reshape(-1, wide)


def body(matrix):
    grid = Grid()
    local_rows, local_cols = matrix.shape
    chunks = 2
    width = local_cols // chunks
    row_slot = jnp.arange(local_rows, dtype=jnp.int32)
    natural_rows = ((row_slot // NB * grid.rows + grid.row) * NB + row_slot % NB)[:, None]
    zero = jnp.float32(0.0)

    def below(value, panel):
        return jnp.where(natural_rows >= (panel + 1) * NB, value, zero)

    def both(a, b):
        return jnp.concatenate([a, b], axis=0)

    mine = matrix[:, :NB]
    other = grid.swap(mine, "col", 1)
    first = grid.col % CORES == 0
    p0, came = grid.from_chip_zero(below(jnp.where(first, mine, other), 0))
    gather = grid.to_columns(p0, chunks)
    b1, _ = grid.from_chip_zero(jnp.where(first, other, mine), (came,))

    p0c = []
    y0 = ()
    for i in range(chunks):
        p0c.append(gather[i].columns(*y0))
        y0 = (product(matrix, p0c[i], i, y0),)
    gram = contract(p0c[0], p0c[0], 0, 0) + contract(p0c[1], p0c[1], 0, 0)
    small = both(gram, jnp.where(grid.col == 1, p0c[0][:NB], zero))
    small = small + grid.swap(small, "col", 1)
    small = grid.add_over(after(small, y0[0]), "col", CORES)
    gram0, p0_one = small[:NB], small[NB:]
    half, part = grid.sum_half(y0[0])
    corner = jnp.where((grid.row == 1) & first, part[:NB], zero)
    small = grid.add_all(both(contract(grid.own_half(p0) * SCALE, part, 0, 0), corner))
    t0 = inverse_factor(gram0, (part,))
    y0 = grid.join_cores(half)
    w0 = contract(p0, t0, 1, 0)
    w0_one = contract(p0_one, t0, 1, 0)
    m0, y0_one = contract(contract(t0 / SCALE, small[:NB], 0, 0), t0, 1, 0), small[NB:]

    def coupled(w, y):
        return 2.0 * contract(t0, y, 0, 0) - 4.0 * contract(m0, w, 1, 0), 2.0 * contract(t0, w, 1, 0)

    for_w, for_y = coupled(w0_one.T, y0_one.T)
    p1 = below(b1 - contract(w0, for_w, 1, 0) - contract(y0, for_y, 1, 0), 1)
    gather = grid.to_columns(p1, chunks)
    (gather_y,) = grid.to_columns(after(y0, gather[-1].distant), 1)
    w0c = [contract(part, t0, 1, 0) for part in p0c]
    p1c = []
    r1 = ()
    waits = ((), (gather_y.first,))
    for i in range(chunks):
        p1c.append(gather[i].columns(*r1))
        r1 = (product(matrix, p1c[i], i, r1, waits[i]),)
    small = sum(both(contract(p1c[i], p1c[i], 0, 0), contract(w0c[i], p1c[i], 0, 0)) for i in range(chunks))
    small = small + grid.swap(small, "col", 1)
    small = grid.add_over(after(small, r1[0]), "col", CORES)
    gram1, w_p = small[:NB], small[NB:]
    half, part = grid.sum_half(r1[0], gather_y.direct)
    sides = jnp.concatenate([grid.own_half(p1), grid.own_half(p0)], axis=1) * SCALE
    small = grid.add_all(contract(sides, part, 0, 0))
    t1 = inverse_factor(gram1, (part,))
    r1 = grid.join_cores(after(half, gather_y.distant, gather_y.crossed[0]))
    gather = grid.to_columns(r1, chunks)

    y_p = small[NB:] / SCALE
    back_w, back_y = coupled(w_p, y_p)
    taken = contract(w_p, back_w, 0, 0) + contract(y_p, back_y, 0, 0)
    m1 = contract(contract(t1 / SCALE, small[:NB] - SCALE * taken, 0, 0), t1, 1, 0)
    y1 = r1 - contract(w0, back_w, 1, 0) - contract(y0, back_y, 1, 0)
    w1 = contract(p1, t1, 1, 0)
    x1 = contract(y1, t1, 1, 0)
    for_r = 2.0 * contract(w1, t1, 1, 1)
    for_p = contract(2.0 * x1 - 4.0 * contract(w1, m1, 1, 0), t1, 1, 1)
    to_w = 2.0 * contract(y0, t0, 1, 0) - 4.0 * contract(w0, m0, 1, 0) - contract(for_r, back_w, 1, 1)
    to_y = 2.0 * contract(w0, t0, 1, 1) - contract(for_r, back_y, 1, 1)
    y0c = gather_y.columns()
    updated = ()
    for i in range(chunks):
        rights = (w0c[i], y0c[i * width : (i + 1) * width], p1c[i], gather[i].columns(*updated))
        updated = (subtract(matrix, i, (to_w, to_y, for_p, for_r), rights, updated),)
    return updated[0]


def solution(mesh):
    placed = (P("row", "col"),)
    return jax.shard_map(
        body, mesh=mesh, in_specs=placed, out_specs=P("row", "col"), check_vma=False
    )
```

time: 403 us -> 367 us (0.911)
  waiting for transfers between devices: 142 us -> 114 us
  Pallas kernels: 113 us -> 92.8 us
  between operations: 6.82 us -> 14.2 us
  local copies, waits for them, and re-layouts: 6.7 us -> 12.1 us
    ppermute x21 -> x23, waiting for transfers between devices: 57.9 us -> 27.5 us  [swap(): return lax.ppermute(value, axis, [(i, i ^ bit) for i in range(size)])]
    pallas_call x10 -> x8, Pallas kernels: 113 us -> 92.8 us  [the longest x2 41 us: subtract(): pl.pallas_call(functools.partial(subtract_kernel, count), grid=(rows // t...]
    slice x8 -> x19, local copies, waits for them, and re-layouts: 4.11 us -> 10.6 us  [after(): return value + jnp.float32(0.0) * sum((other[0, 0] for other in others))]
    ppermute x21 -> x23, starting transfers between devices: 21.1 us -> 27.6 us  [swap(): return lax.ppermute(value, axis, [(i, i ^ bit) for i in range(size)])]
    ppermute x44, starting transfers between devices: 63.9 us -> 58 us  [send(): return lax.ppermute(value, AXES, pairs)]
    dot_general x35 -> x38, matrix products: 32 us -> 34.7 us  [contract(): lax.dot_general(left, right, (((left_dim,), (right_dim,)), ((), ())), pre...]
  transfers between devices with their start and end apart: 65 -> 67, of which waited for: 28 -> 25; matrix products, arithmetic and copies ran while one was open for 10% -> 14% of each run, Pallas kernels for 19% -> 20%
where the time goes in v1:
time: 367 us; the launch traced here: 360 us
  waiting for transfers between devices  114 us (31%)
  Pallas kernels  92.8 us (25%)
  starting transfers between devices  85.6 us (23%)
  matrix products  34.7 us (9%)
  between operations  14.2 us (4%)
  local copies, waits for them, and re-layouts  12.1 us (3%)
  other arithmetic  6.76 us (2%)
    ppermute x44, waiting for transfers between devices, send(): return lax.ppermute(value, AXES, pairs)  86.9 us
    ppermute x44, starting transfers between devices, send(): return lax.ppermute(value, AXES, pairs)  58 us
    pallas_call x2, Pallas kernels, subtract(): pl.pallas_call(functools.partial(subtract_kernel, count), grid=(rows // t...  41 us
    pallas_call x4, Pallas kernels, product(): pl.pallas_call(functools.partial(product_kernel, len(before)), grid=(rows...  34.9 us
    dot_general x38, matrix products, contract(): lax.dot_general(left, right, (((left_dim,), (right_dim,)), ((), ())), pre...  34.7 us
    ppermute x23, starting transfers between devices, swap(): return lax.ppermute(value, axis, [(i, i ^ bit) for i in range(size)])  27.6 us
    ppermute x23, waiting for transfers between devices, swap(): return lax.ppermute(value, axis, [(i, i ^ bit) for i in range(size)])  27.5 us
    pallas_call x2, Pallas kernels, inverse_factor(): pl.pallas_call(factor_kernel, in_specs=[pl.BlockSpec((NB, NB), lambda: (0...  16.9 us
  transfers between devices with their start and end apart: 67, of which 25 were waited for; matrix products, arithmetic and copies ran while one was open for 14% of the time, Pallas kernels for 20%

profile of v1, /device:TPU:4, one launch (start us, length us, event | category | flops | bytes accessed | tf_op | source)
XLA Modules:
  0.0 360.4 jit_solution(8503119299197335263)
XLA Ops:
  5.5 14.5 %collective-permute-done.1 = f32[1024,128]{1,0:T(8,128)S(1)} collective-permute-done((f32[1024,128]{1,0:T(8,128)S(1)}, f32[1024,128]{1,0:T(8,128)S(1)}, u32[]{:S(2)}, u32[]{:S(2)}) %collective-permute-start.1) | collective-permute-done | bytes 524320 | tf_op jit(solution)/shard_map/ppermute | solution.py:220
  29.4 3.9 %collective-permute-done.3 = f32[1024,128]{1,0:T(8,128)S(1)} collective-permute-done((f32[1024,128]{1,0:T(8,128)S(1)}, f32[1024,128]{1,0:T(8,128)S(1)}, u32[]{:S(2)}, u32[]{:S(2)}) %collective-permute-start.3) | collective-permute-done | bytes 524320 | tf_op jit(solution)/shard_map/ppermute | solution.py:220
  38.9 11.3 %collective-permute-done.8 = f32[1024,128]{1,0:T(8,128)S(1)} collective-permute-done((f32[1024,128]{1,0:T(8,128)}, f32[1024,128]{1,0:T(8,128)S(1)}, u32[]{:S(2)}, u32[]{:S(2)}) %collective-permute-start.8) | collective-permute-done | bytes 524320 | tf_op jit(solution)/shard_map/ppermute | solution.py:220
  59.4 4.4 %collective-permute-start.6 = (f32[1024,128]{1,0:T(8,128)S(1)}, f32[1024,128]{1,0:T(8,128)S(1)}, u32[]{:S(2)}, u32[]{:S(2)}) collective-permute-start(f32[1024,128]{1,0:T(8,128)S(1)} %add_select_fusion.8), channel_id=1, source_target_pairs={{0,4},{5,1},{2,6},{7,3},{8,12},{13,9},{10,14},{15,11},{16,20},{21,... | collective-permute-start | bytes 1572872 | tf_op jit(solution)/shard_map/ppermute | solution.py:220
  65.2 4.3 %collective-permute-start.14 = (f32[1024,128]{1,0:T(8,128)S(1)}, f32[1024,128]{1,0:T(8,128)S(1)}, u32[]{:S(2)}, u32[]{:S(2)}) collective-permute-start(f32[1024,128]{1,0:T(8,128)S(1)} %add_add_fusion.7), channel_id=1, source_target_pairs={{0,4},{5,1},{2,6},{7,3},{8,12},{13,9},{10,14},{15,11},{16,20},{21,... | collective-permute-start | bytes 1572872 | tf_op jit(solution)/shard_map/ppermute | solution.py:220
  69.7 8.6 %product.4.refs_0_ = f32[2048,128]{1,0:T(8,128)S(1)} custom-call(f32[2048,4096]{1,0:T(8,128)} %a_ref.11, f32[2048,128]{1,0:T(8,128)S(1)} %bitcast.142), custom_call_target="tpu_custom_call" | custom-call | flops 4294967296 | bytes 16777216 | tf_op jit(solution)/shard_map/product/pallas_call | solution.py:90
  79.7 8.9 %product.5 = f32[2048,128]{1,0:T(8,128)S(1)} custom-call(f32[2048,4096]{1,0:T(8,128)} %a_ref.11, f32[2048,128]{1,0:T(8,128)S(1)} %bitcast.145, f32[2048,128]{1,0:T(8,128)S(1)} %product.4.refs_0_), custom_call_target="tpu_custom_call" | custom-call | flops 4294967296 | bytes 16777216 | tf_op jit(solution)/shard_map/product/pallas_call | solution.py:90
  95.5 5.3 %collective-permute-done.20 = f32[256,128]{1,0:T(8,128)S(1)} collective-permute-done((f32[256,128]{1,0:T(8,128)S(1)}, f32[256,128]{1,0:T(8,128)S(1)}, u32[]{:S(2)}, u32[]{:S(2)}) %collective-permute-start.20) | collective-permute-done | bytes 131104 | tf_op jit(solution)/shard_map/ppermute | solution.py:224
  101.4 8.4 %factor.2 = f32[128,128]{1,0:T(8,128)S(1)} custom-call(f32[128,128]{1,0:T(8,128)S(1)} %slice.153.gram_ref, f32[1024,128]{1,0:T(8,128)S(1)} %dynamic-slice_add_fusion.refs_0_), custom_call_target="tpu_custom_call" | custom-call | flops 8388608 | bytes 131072 | tf_op jit(solution)/shard_map/factor/pallas_call | solution.py:189
  112.8 5.6 %collective-permute-done.22 = f32[256,128]{1,0:T(8,128)S(1)} collective-permute-done((f32[256,128]{1,0:T(8,128)S(1)}, f32[256,128]{1,0:T(8,128)S(1)}, u32[]{:S(2)}, u32[]{:S(2)}) %collective-permute-start.22) | collective-permute-done | bytes 131104 | tf_op jit(solution)/shard_map/ppermute | solution.py:224
  120.1 3.3 collective-permute-done.23
  132.4 7.4 %collective-permute-done.27 = f32[1024,128]{1,0:T(8,128)S(1)} collective-permute-done((f32[1024,128]{1,0:T(8,128)S(1)}, f32[1024,128]{1,0:T(8,128)S(1)}, u32[]{:S(2)}, u32[]{:S(2)}) %collective-permute-start.27) | collective-permute-done | bytes 524320 | tf_op jit(solution)/shard_map/ppermute | solution.py:220
  147.4 6.0 %collective-permute-done.30 = f32[1024,128]{1,0:T(8,128)S(1)} collective-permute-done((f32[1024,128]{1,0:T(8,128)S(1)}, f32[1024,128]{1,0:T(8,128)S(1)}, u32[]{:S(2)}, u32[]{:S(2)}) %collective-permute-start.30) | collective-permute-done | bytes 524320 | tf_op jit(solution)/shard_map/ppermute | solution.py:220
  162.6 4.2 %collective-permute-done.36 = f32[1024,128]{1,0:T(8,128)S(1)} collective-permute-done((f32[1024,128]{1,0:T(8,128)S(1)}, f32[1024,128]{1,0:T(8,128)S(1)}, u32[]{:S(2)}, u32[]{:S(2)}) %collective-permute-start.36) | collective-permute-done | bytes 524320 | tf_op jit(solution)/shard_map/ppermute | solution.py:220
  172.4 8.8 %product.6.refs_0_ = f32[2048,128]{1,0:T(8,128)S(1)} custom-call(f32[2048,4096]{1,0:T(8,128)} %a_ref.11, f32[2048,128]{1,0:T(8,128)S(1)} %bitcast.136), custom_call_target="tpu_custom_call" | custom-call | flops 4294967296 | bytes 16777216 | tf_op jit(solution)/shard_map/product/pallas_call | solution.py:90
  191.5 8.6 %product.7 = f32[2048,128]{1,0:T(8,128)S(1)} custom-call(f32[2048,4096]{1,0:T(8,128)} %a_ref.11, f32[2048,128]{1,0:T(8,128)S(1)} %bitcast.140, f32[2048,128]{1,0:T(8,128)S(1)} %product.6.refs_0_, f32[2048,128]{1,0:T(8,128)S(1)} %collective-permute-done.40.refs_1_), custom_call_target="tpu_custom_call" | custom-call | flops 4294967296 | bytes 16777216 | tf_op jit(solution)/shard_map/product/pallas_call | solution.py:90
  202.5 10.5 %collective-permute-start.41 = (f32[256,128]{1,0:T(8,128)S(1)}, f32[256,128]{1,0:T(8,128)S(1)}, u32[]{:S(2)}, u32[]{:S(2)}) collective-permute-start(f32[256,128]{1,0:T(8,128)S(1)} %add_add_fusion.9), channel_id=1, source_target_pairs={{0,2},{1,3},{2,0},{3,1},{4,6},{5,7},{6,4},{7,5},{8,10},{9,11},{10,... | collective-permute-start | bytes 393224 | tf_op jit(solution)/shard_map/ppermute | solution.py:224
  221.4 8.4 %factor.3 = f32[128,128]{1,0:T(8,128)S(1)} custom-call(f32[128,128]{1,0:T(8,128)S(1)} %slice.167.gram_ref, f32[1024,128]{1,0:T(8,128)S(1)} %add_add_fusion.4.refs_0_), custom_call_target="tpu_custom_call" | custom-call | flops 8388608 | bytes 131072 | tf_op jit(solution)/shard_map/factor/pallas_call | solution.py:189
  246.5 4.3 %collective-permute-start.47 = (f32[256,128]{1,0:T(8,128)S(1)}, f32[256,128]{1,0:T(8,128)S(1)}, u32[]{:S(2)}, u32[]{:S(2)}) collective-permute-start(f32[256,128]{1,0:T(8,128)S(1)} %add.415), channel_id=1, source_target_pairs={{0,2},{1,3},{2,0},{3,1},{4,6},{5,7},{6,4},{7,5},{8,10},{9,11},{10,... | collective-permute-start | bytes 393224 | tf_op jit(solution)/shard_map/ppermute | solution.py:224
  267.4 8.9 %collective-permute-done.55 = f32[1024,128]{1,0:T(8,128)S(1)} collective-permute-done((f32[1024,128]{1,0:T(8,128)S(1)}, f32[1024,128]{1,0:T(8,128)S(1)}, u32[]{:S(2)}, u32[]{:S(2)}) %collective-permute-start.55) | collective-permute-done | bytes 524320 | tf_op jit(solution)/shard_map/ppermute | solution.py:220
  284.0 18.7 %collective-permute-done.60 = f32[1024,128]{1,0:T(8,128)S(1)} collective-permute-done((f32[1024,128]{1,0:T(8,128)S(1)}, f32[1024,128]{1,0:T(8,128)S(1)}, u32[]{:S(2)}, u32[]{:S(2)}) %collective-permute-start.60) | collective-permute-done | bytes 524320 | tf_op jit(solution)/shard_map/ppermute | solution.py:220
  312.0 3.3 collective-permute-done.64
  317.1 20.5 %subtract.2.refs_8_ = f32[2048,4096]{1,0:T(8,128)} custom-call(f32[2048,4096]{1,0:T(8,128)} %a_ref.11, f32[2048,128]{1,0:T(8,128)S(1)} %fusion.3.refs_0_, f32[2048,128]{1,0:T(8,128)S(1)} %fusion.1.refs_1_, f32[2048,128]{1,0:T(8,128)S(1)} %fusion.77.refs_2_, f32[2048,128]{1,0:T(8,128)S(1)} %convolution_multiply_fusion.3.refs_3_, ...), custom_call_target="tpu_custom_call" | custom-call | flops 12884901888 | bytes 33554432 | tf_op jit(solution)/shard_map/subtract/pallas_call | solution.py:131
  339.8 20.5 %subtract.3 = f32[2048,4096]{1,0:T(8,128)} custom-call(f32[2048,4096]{1,0:T(8,128)} %a_ref.11, f32[2048,128]{1,0:T(8,128)S(1)} %fusion.3.refs_0_, f32[2048,128]{1,0:T(8,128)S(1)} %fusion.1.refs_1_, f32[2048,128]{1,0:T(8,128)S(1)} %fusion.77.refs_2_, f32[2048,128]{1,0:T(8,128)S(1)} %convolution_multiply_fusion.3.refs_3_, ...), custom_call_target="tpu_custom_call", output_to_operand_aliasing={{}: (9, {})} | custom-call | flops 12884901888 | bytes 33554432 | tf_op jit(solution)/shard_map/subtract/pallas_call | solution.py:131
  (248 shorter events, 137.5 us)
Async XLA Ops:
  27.4 25.3 %collective-permute-start.25 = (f32[1024,128]{1,0:T(8,128)S(1)}, f32[1024,128]{1,0:T(8,128)S(1)}, u32[]{:S(2)}, u32[]{:S(2)}) collective-permute-start(f32[1024,128]{1,0:T(8,128)S(1)} %select_add_fusion.1), channel_id=1, source_target_pairs={{0,2},{1,3},{4,6},{5,7},{8,10},{9,11},{12,14},{13,15},{16,18},{17,... | collective-permute-start | bytes 1572872 | tf_op jit(solution)/shard_map/ppermute | solution.py:220
  35.8 29.2 %collective-permute-start.13 = (f32[1024,128]{1,0:T(8,128)S(1)}, f32[1024,128]{1,0:T(8,128)S(1)}, u32[]{:S(2)}, u32[]{:S(2)}) collective-permute-start(f32[1024,128]{1,0:T(8,128)S(1)} %get-tuple-element.7), channel_id=1, source_target_pairs={{16,8},{21,13},{10,18},{15,23}} | collective-permute-start | bytes 1572872 | tf_op jit(solution)/shard_map/ppermute | solution.py:220
  36.5 17.5 %collective-permute-start.11 = (f32[1024,128]{1,0:T(8,128)S(1)}, f32[1024,128]{1,0:T(8,128)S(1)}, u32[]{:S(2)}, u32[]{:S(2)}) collective-permute-start(f32[1024,128]{1,0:T(8,128)S(1)} %get-tuple-element.7), channel_id=1, source_target_pairs={{0,16},{16,0},{5,21},{21,5},{26,10},{10,26},{31,15},{15,31}} | collective-permute-start | bytes 1572872 | tf_op jit(solution)/shard_map/ppermute | solution.py:220
  37.6 21.8 %collective-permute-start.4 = (f32[1024,128]{1,0:T(8,128)S(1)}, f32[1024,128]{1,0:T(8,128)S(1)}, u32[]{:S(2)}, u32[]{:S(2)}) collective-permute-start(f32[1024,128]{1,0:T(8,128)S(1)} %get-tuple-element.7), channel_id=1, source_target_pairs={{0,8},{16,24},{5,13},{21,29},{26,18},{10,2},{31,23},{15,7}} | collective-permute-start | bytes 1572872 | tf_op jit(solution)/shard_map/ppermute | solution.py:220
  58.2 42.7 %collective-permute-start.26 = (f32[1024,128]{1,0:T(8,128)S(1)}, f32[1024,128]{1,0:T(8,128)S(1)}, u32[]{:S(2)}, u32[]{:S(2)}) collective-permute-start(f32[1024,128]{1,0:T(8,128)S(1)} %select_add_fusion), channel_id=1, source_target_pairs={{0,1},{1,0},{2,3},{3,2},{4,5},{5,4},{6,7},{7,6},{8,9},{9,8},{10,11... | collective-permute-start | bytes 1572872 | tf_op jit(solution)/shard_map/ppermute | solution.py:224
  59.4 20.1 %collective-permute-start.6 = (f32[1024,128]{1,0:T(8,128)S(1)}, f32[1024,128]{1,0:T(8,128)S(1)}, u32[]{:S(2)}, u32[]{:S(2)}) collective-permute-start(f32[1024,128]{1,0:T(8,128)S(1)} %add_select_fusion.8), channel_id=1, source_target_pairs={{0,4},{5,1},{2,6},{7,3},{8,12},{13,9},{10,14},{15,11},{16,20},{21,... | collective-permute-start | bytes 1572872 | tf_op jit(solution)/shard_map/ppermute | solution.py:220
  101.1 22.8 %collective-permute-start.16 = (f32[1024,128]{1,0:T(8,128)S(1)}, f32[1024,128]{1,0:T(8,128)S(1)}, u32[]{:S(2)}, u32[]{:S(2)}) collective-permute-start(f32[1024,128]{1,0:T(8,128)S(1)} %dynamic-slice_add_fusion.refs_0_), channel_id=1, source_target_pairs={{0,2},{1,3},{2,0},{3,1},{4,6},{5,7},{6,4},{7,5},{8,10},{9,11},{10,... | collective-permute-start | bytes 1572872 | tf_op jit(solution)/shard_map/ppermute | solution.py:224
  144.1 18.5 %collective-permute-start.37 = (f32[1024,128]{1,0:T(8,128)S(1)}, f32[1024,128]{1,0:T(8,128)S(1)}, u32[]{:S(2)}, u32[]{:S(2)}) collective-permute-start(f32[1024,128]{1,0:T(8,128)S(1)} %get-tuple-element.27), channel_id=1, source_target_pairs={{16,8},{21,13},{10,18},{15,23}} | collective-permute-start | bytes 1572872 | tf_op jit(solution)/shard_map/ppermute | solution.py:220
  159.1 26.9 %collective-permute-start.34 = (f32[1024,128]{1,0:T(8,128)S(1)}, f32[1024,128]{1,0:T(8,128)S(1)}, u32[]{:S(2)}, u32[]{:S(2)}) collective-permute-start(f32[1024,128]{1,0:T(8,128)S(1)} %add_select_fusion.5), channel_id=1, source_target_pairs={{0,4},{5,1},{2,6},{7,3},{8,12},{13,9},{10,14},{15,11},{16,20},{21,... | collective-permute-start | bytes 1572872 | tf_op jit(solution)/shard_map/ppermute | solution.py:220
  167.4 18.7 %collective-permute-start.38 = (f32[1024,128]{1,0:T(8,128)S(1)}, f32[1024,128]{1,0:T(8,128)S(1)}, u32[]{:S(2)}, u32[]{:S(2)}) collective-permute-start(f32[1024,128]{1,0:T(8,128)S(1)} %add_add_fusion.5), channel_id=1, source_target_pairs={{0,4},{5,1},{2,6},{7,3},{8,12},{13,9},{10,14},{15,11},{16,20},{21,... | collective-permute-start | bytes 1572872 | tf_op jit(solution)/shard_map/ppermute | solution.py:220
  169.4 81.4 %collective-permute-start.51 = (f32[2048,128]{1,0:T(8,128)S(1)}, f32[2048,128]{1,0:T(8,128)S(1)}, u32[]{:S(2)}, u32[]{:S(2)}) collective-permute-start(f32[2048,128]{1,0:T(8,128)S(1)} %broadcast_add_fusion), channel_id=1, source_target_pairs={{16,8},{21,13},{10,18},{15,23}} | collective-permute-start | bytes 3145736 | tf_op jit(solution)/shard_map/ppermute | solution.py:220
  170.2 29.9 %collective-permute-start.43 = (f32[2048,128]{1,0:T(8,128)S(1)}, f32[2048,128]{1,0:T(8,128)S(1)}, u32[]{:S(2)}, u32[]{:S(2)}) collective-permute-start(f32[2048,128]{1,0:T(8,128)S(1)} %broadcast_add_fusion), channel_id=1, source_target_pairs={{0,16},{16,0},{5,21},{21,5},{26,10},{10,26},{31,15},{15,31}} | collective-permute-start | bytes 3145736 | tf_op jit(solution)/shard_map/ppermute | solution.py:220
  170.9 20.6 %collective-permute-start.40 = (f32[2048,128]{1,0:T(8,128)S(1)}, f32[2048,128]{1,0:T(8,128)S(1)}, u32[]{:S(2)}, u32[]{:S(2)}) collective-permute-start(f32[2048,128]{1,0:T(8,128)S(1)} %broadcast_add_fusion), channel_id=1, source_target_pairs={{0,8},{16,24},{5,13},{21,29},{26,18},{10,2},{31,23},{15,7}} | collective-permute-start | bytes 3145736 | tf_op jit(solution)/shard_map/ppermute | solution.py:220
  213.1 41.5 %collective-permute-start.52 = (f32[2048,128]{1,0:T(8,128)S(1)}, f32[2048,128]{1,0:T(8,128)S(1)}, u32[]{:S(2)}, u32[]{:S(2)}) collective-permute-start(f32[2048,128]{1,0:T(8,128)S(1)} %broadcast_select_fusion.4), channel_id=1, source_target_pairs={{0,4},{5,1},{2,6},{7,3},{8,12},{13,9},{10,14},{15,11},{16,20},{21,... | collective-permute-start | bytes 3145736 | tf_op jit(solution)/shard_map/ppermute | solution.py:220
  214.5 36.4 %collective-permute-start.50 = (f32[2048,128]{1,0:T(8,128)S(1)}, f32[2048,128]{1,0:T(8,128)S(1)}, u32[]{:S(2)}, u32[]{:S(2)}) collective-permute-start(f32[2048,128]{1,0:T(8,128)S(1)} %collective-permute-done.43), channel_id=1, source_target_pairs={{16,24},{21,29},{10,2},{15,7}} | collective-permute-start | bytes 3145736 | tf_op jit(solution)/shard_map/ppermute | solution.py:220
  217.5 39.1 %collective-permute-start.49 = (f32[1024,128]{1,0:T(8,128)S(1)}, f32[1024,128]{1,0:T(8,128)S(1)}, u32[]{:S(2)}, u32[]{:S(2)}) collective-permute-start(f32[1024,128]{1,0:T(8,128)S(1)} %add_add_fusion.4.refs_0_), channel_id=1, source_target_pairs={{0,2},{1,3},{2,0},{3,1},{4,6},{5,7},{6,4},{7,5},{8,10},{9,11},{10,... | collective-permute-start | bytes 1572872 | tf_op jit(solution)/shard_map/ppermute | solution.py:224
  263.4 19.3 %collective-permute-start.61 = (f32[1024,128]{1,0:T(8,128)S(1)}, f32[1024,128]{1,0:T(8,128)S(1)}, u32[]{:S(2)}, u32[]{:S(2)}) collective-permute-start(f32[1024,128]{1,0:T(8,128)S(1)} %broadcast_select_fusion.27), channel_id=1, source_target_pairs={{16,8},{21,13},{10,18},{15,23}} | collective-permute-start | bytes 1572872 | tf_op jit(solution)/shard_map/ppermute | solution.py:220
  277.6 34.4 %collective-permute-start.65 = (f32[1024,128]{1,0:T(8,128)S(1)}, f32[1024,128]{1,0:T(8,128)S(1)}, u32[]{:S(2)}, u32[]{:S(2)}) collective-permute-start(f32[1024,128]{1,0:T(8,128)S(1)} %get-tuple-element.5), channel_id=1, source_target_pairs={{16,8},{21,13},{10,18},{15,23}} | collective-permute-start | bytes 1572872 | tf_op jit(solution)/shard_map/ppermute | solution.py:220
  278.3 25.9 %collective-permute-start.63 = (f32[1024,128]{1,0:T(8,128)S(1)}, f32[1024,128]{1,0:T(8,128)S(1)}, u32[]{:S(2)}, u32[]{:S(2)}) collective-permute-start(f32[1024,128]{1,0:T(8,128)S(1)} %get-tuple-element.5), channel_id=1, source_target_pairs={{0,16},{16,0},{5,21},{21,5},{26,10},{10,26},{31,15},{15,31}} | collective-permute-start | bytes 1572872 | tf_op jit(solution)/shard_map/ppermute | solution.py:220
  279.0 28.7 %collective-permute-start.56 = (f32[1024,128]{1,0:T(8,128)S(1)}, f32[1024,128]{1,0:T(8,128)S(1)}, u32[]{:S(2)}, u32[]{:S(2)}) collective-permute-start(f32[1024,128]{1,0:T(8,128)S(1)} %get-tuple-element.5), channel_id=1, source_target_pairs={{0,8},{16,24},{5,13},{21,29},{26,18},{10,2},{31,23},{15,7}} | collective-permute-start | bytes 1572872 | tf_op jit(solution)/shard_map/ppermute | solution.py:220
  280.3 22.5 %collective-permute-start.60 = (f32[1024,128]{1,0:T(8,128)S(1)}, f32[1024,128]{1,0:T(8,128)S(1)}, u32[]{:S(2)}, u32[]{:S(2)}) collective-permute-start(f32[1024,128]{1,0:T(8,128)S(1)} %collective-permute-done.59), channel_id=1, source_target_pairs={{16,24},{21,29},{10,2},{15,7}} | collective-permute-start | bytes 1572872 | tf_op jit(solution)/shard_map/ppermute | solution.py:220
  282.7 23.8 %collective-permute-start.57 = (f32[1024,128]{1,0:T(8,128)S(1)}, f32[1024,128]{1,0:T(8,128)S(1)}, u32[]{:S(2)}, u32[]{:S(2)}) collective-permute-start(f32[1024,128]{1,0:T(8,128)S(1)} %broadcast_select_fusion.11), channel_id=1, source_target_pairs={{0,4},{5,1},{2,6},{7,3},{8,12},{13,9},{10,14},{15,11},{16,20},{21,... | collective-permute-start | bytes 1572872 | tf_op jit(solution)/shard_map/ppermute | solution.py:220
  307.7 31.8 %collective-permute-start.58 = (f32[1024,128]{1,0:T(8,128)S(1)}, f32[1024,128]{1,0:T(8,128)S(1)}, u32[]{:S(2)}, u32[]{:S(2)}) collective-permute-start(f32[1024,128]{1,0:T(8,128)S(1)} %add_select_fusion.2), channel_id=1, source_target_pairs={{0,4},{5,1},{2,6},{7,3},{8,12},{13,9},{10,14},{15,11},{16,20},{21,... | collective-permute-start | bytes 1572872 | tf_op jit(solution)/shard_map/ppermute | solution.py:220
  315.4 24.2 %collective-permute-start.66 = (f32[1024,128]{1,0:T(8,128)S(1)}, f32[1024,128]{1,0:T(8,128)S(1)}, u32[]{:S(2)}, u32[]{:S(2)}) collective-permute-start(f32[1024,128]{1,0:T(8,128)S(1)} %add_add_fusion.1), channel_id=1, source_target_pairs={{0,4},{5,1},{2,6},{7,3},{8,12},{13,9},{10,14},{15,11},{16,20},{21,... | collective-permute-start | bytes 1572872 | tf_op jit(solution)/shard_map/ppermute | solution.py:220
  (44 other events, 392.9 us)
